TPU v7x, 256 devices: a whole 4x4x8 slice. The times are simulated.
256 devices in a mesh: seq: 32 (over y, x, core), dp: 8 (over z).
Axes of the slice: x: 4, y: 4, z: 8, core: 2. Of those that a mesh axis runs over, the one named last changes fastest.
Arguments:
- tokens: bfloat16 [8, 8192, 2048], P('dp', 'seq'), may hold values from -6 to 6
- w_qkv: bfloat16 [2048, 3, 1024], P('seq'), may hold values from -0.125 to 0.125
- weight_table: float32 [16, 8], replicated, may hold values from 0.3 to 3
- weight_index: int32 [8, 64, 6], P('dp', 'seq'), may hold values from 0 to 15
- cotangent: bfloat16 [8, 8192, 1024], P('dp', 'seq'), may hold values from -6 to 6
Outputs:
- attn_out: bfloat16 [8, 8192, 1024], P('dp', 'seq')
- grad_w: float32 [2048, 3, 1024], P('seq')
All inputs are finite; a program needn't handle non-finite values.
Results may differ from a plain program's by a relative error of at most 0.02.
Values may be sent and summed in bfloat16 or wider, within the bound.
No kernel may reach another device: no remote copies, remote signals or barrier semaphores. Data moves between devices by JAX's collectives and lax.ppermute only.
A program may use at most 128 MiB of HBM per device.

v0:
```python
import math
import jax
import jax.numpy as jnp
from jax import lax
from jax.sharding import PartitionSpec as P


def swapped(value, axis, bit):
    mask = 2**bit
    pairs = [(source, source ^ mask) for source in range(lax.axis_size(axis))]
    return lax.ppermute(value, axis, pairs)


def level_factors(weight_table, weight_index, block_len):
    table_rows = weight_table.shape[0]
    chosen = weight_index[0]
    onehot = (chosen[:, :, None] == jnp.arange(table_rows, dtype=jnp.int32)[None, None, :]).astype(
        jnp.float32
    )
    per_block = jnp.einsum("blw,wh->blh", onehot, weight_table, precision=lax.Precision.HIGHEST)
    groups = chosen.shape[0]
    spread = jnp.broadcast_to(
        per_block[:, None], (groups, block_len // groups, chosen.shape[1], weight_table.shape[1])
    )
    return spread.reshape(block_len, chosen.shape[1], weight_table.shape[1])


def make_adder(inputs, columns, shard_rows):
    flat_rows = shard_rows.reshape(shard_rows.shape[0], columns)
    return jnp.dot(inputs, flat_rows, preferred_element_type=jnp.float32)


def climb(keys_bf, values_bf, levels):
    running = jnp.einsum("shd,she->hde", keys_bf, values_bf, preferred_element_type=jnp.float32)
    partners = []
    for bit_pos in range(levels):
        partner = swapped(running.astype(jnp.bfloat16), "seq", bit_pos).astype(running.dtype)
        partners.append(partner)
        running = running + partner
    return partners


def descend(level_grads, levels, device):
    carried = [level_grads[:, bit_pos] for bit_pos in range(levels)]
    gathered = jnp.zeros_like(level_grads[:, 0])
    for bit_pos in range(levels):
        outgoing = jnp.stack(carried[bit_pos:], axis=1)
        incoming = swapped(outgoing.astype(jnp.bfloat16), "seq", bit_pos).astype(outgoing.dtype)
        keeping = (1 - device // 2**bit_pos % 2).astype(jnp.float32)
        gathered = gathered + keeping * incoming[:, 0]
        for upper in range(bit_pos + 1, levels):
            carried[upper] = carried[upper] + incoming[:, upper - bit_pos]
    return gathered


def per_device(tokens, w_qkv, weight_table, weight_index, cotangent):
    inputs = tokens[0]
    block_len = inputs.shape[0]
    inner_width = w_qkv.shape[2]
    head_count = weight_table.shape[1]
    head_dim = inner_width // head_count
    levels = lax.axis_size("seq").bit_length() - 1
    device = lax.axis_index("seq")
    projected = make_adder(
        inputs, 3 * inner_width, lax.all_gather(w_qkv, "seq", axis=0, tiled=True)
    )
    projected = projected.astype(jnp.bfloat16).reshape(block_len, 3, head_count, head_dim)
    queries = projected[:, 0]
    keys_bf = projected[:, 1]
    values_bf = projected[:, 2]
    partners = climb(keys_bf, values_bf, levels)
    level_states = jnp.stack(partners, axis=2).astype(jnp.bfloat16)
    powers = 2 ** jnp.arange(levels, dtype=jnp.int32)
    bit_flags = (device // powers % 2).astype(jnp.float32)
    halves = 2.0 ** jnp.arange(levels, dtype=jnp.float32)
    scale_level = bit_flags / jnp.sqrt(head_dim * halves * block_len)
    weights_tok = level_factors(weight_table, weight_index, block_len)
    level_coef = jnp.transpose(weights_tok[:, 1 : levels + 1, :], (0, 2, 1)) * scale_level
    local_scale = weights_tok[:, 0, :] / math.sqrt(head_dim * block_len)
    row_scale = jnp.transpose(local_scale)[:, :, None]
    causal = jnp.arange(block_len)[:, None] >= jnp.arange(block_len)[None, :]
    raw_scores = jnp.einsum("thd,shd->hts", queries, keys_bf, preferred_element_type=jnp.float32)
    scores = jnp.where(causal[None], raw_scores * row_scale, 0.0).astype(jnp.bfloat16)
    local_out = jnp.einsum("hts,she->the", scores, values_bf, preferred_element_type=jnp.float32)
    far_terms = jnp.einsum(
        "thd,hdle->thle", queries, level_states, preferred_element_type=jnp.float32
    )
    attended = local_out + jnp.sum(far_terms * level_coef[..., None], axis=2)
    attn_out = attended.astype(jnp.bfloat16).reshape(1, block_len, inner_width)
    upstream = cotangent[0].reshape(block_len, head_count, head_dim)
    raw_grads = jnp.einsum("the,she->hts", upstream, values_bf, preferred_element_type=jnp.float32)
    dscores = jnp.where(causal[None], raw_grads * row_scale, 0.0).astype(jnp.bfloat16)
    far_grads = jnp.einsum(
        "the,hdle->thld", upstream, level_states, preferred_element_type=jnp.float32
    )
    grad_q = jnp.einsum("hts,shd->thd", dscores, keys_bf, preferred_element_type=jnp.float32)
    grad_q = grad_q + jnp.sum(far_grads * level_coef[..., None], axis=2)
    grad_k = jnp.einsum("hts,thd->shd", dscores, queries, preferred_element_type=jnp.float32)
    grad_v = jnp.einsum("hts,the->she", scores, upstream, preferred_element_type=jnp.float32)
    scaled = (queries.astype(jnp.float32)[:, :, None, :] * level_coef[..., None]).astype(
        jnp.bfloat16
    )
    level_grads = jnp.einsum("thld,the->hlde", scaled, upstream, preferred_element_type=jnp.float32)
    state_grads = descend(level_grads, levels, device).astype(jnp.bfloat16)
    grad_k = grad_k + jnp.einsum(
        "she,hde->shd", values_bf, state_grads, preferred_element_type=jnp.float32
    )
    grad_v = grad_v + jnp.einsum(
        "shd,hde->she", keys_bf, state_grads, preferred_element_type=jnp.float32
    )
    qkv_grads = (
        jnp.stack([grad_q, grad_k, grad_v], axis=1)
        .astype(jnp.bfloat16)
        .reshape(block_len, 3 * inner_width)
    )
    shard_rows = w_qkv.shape[0]
    partial_value = jnp.einsum("tr,tc->rc", inputs, qkv_grads, preferred_element_type=jnp.float32)
    seq_sum = lax.psum_scatter(
        partial_value.reshape(lax.axis_size("seq") * shard_rows, 3, inner_width).astype(
            jnp.bfloat16
        ),
        "seq",
        scatter_dimension=0,
        tiled=True,
    )
    grad_w = lax.psum(seq_sum, "dp").astype(jnp.float32)
    return (attn_out, grad_w)


def solution(mesh):
    return jax.shard_map(
        per_device,
        mesh=mesh,
        in_specs=(
            P("dp", "seq", None),
            P("seq", None, None),
            P(),
            P("dp", "seq", None),
            P("dp", "seq", None),
        ),
        out_specs=(P("dp", "seq", None), P("seq", None, None)),
        check_vma=False,
    )
```

profile of v0, /device:TPU:2, one launch (start us, length us, event | category | flops | bytes accessed | tf_op | source)
XLA Modules:
  0.0 420.0 jit_solution(265844752788603229)
XLA Ops:
  9.2 1.1 copy.96
  10.4 71.2 %all-gather.2.cloned.1.call-done = bf16[2048,3,1024]{2,0,1:T(8,128)(2,1)} async-done(((bf16[64,3,1024]{2,0,1:T(8,128)(2,1)}), bf16[2048,3,1024]{2,0,1:T(8,128)(2,1)}) %all-gather.2.cloned.1.call-update) | async-done | bytes 12582928 | tf_op jit(solution)/shard_map/all_gather | solution.py:65
  81.5 17.0 %copy.52 = bf16[2048,3,1024]{0,2,1:T(8,128)(2,1)} copy(bf16[2048,3,1024]{2,0,1:T(8,128)(2,1)} %all-gather.2.cloned.1.call-done) | data formatting | bytes 25165824 | tf_op jit(solution)/shard_map/all_gather | solution.py:65
  98.5 8.0 %fusion.6 = bf16[32,8,24,128]{3,1,2,0:T(8,128)(2,1)S(1)} fusion(bf16[2048,3072]{0,1:T(8,128)(2,1)} %bitcast.131, bf16[1,256,2048]{2,1,0:T(8,128)(2,1)S(1)} %copy-done), kind=kOutput, calls=%fused_computation.14 | convolution fusion | flops 3222011904 | bytes 15204352 | tf_op jit(solution)/shard_map/dot_general | solution.py:30
  108.9 2.5 copy.68
  111.5 3.9 fusion.67
  116.8 1.3 copy.92
  119.7 1.8 convert_element_type.144
  123.6 1.5 collective-permute-start.1
  125.5 27.9 %collective-permute-done.1 = bf16[8,128,128]{2,1,0:T(8,128)(2,1)S(1)} collective-permute-done((bf16[8,128,128]{2,1,0:T(8,128)(2,1)S(1)}, bf16[8,128,128]{2,1,0:T(8,128)(2,1)S(1)}, u32[]{:S(2)}, u32[]{:S(2)}) %collective-permute-start.1) | collective-permute-done | bytes 262176 | tf_op jit(solution)/shard_map/ppermute | solution.py:11
  153.4 2.4 collective-permute-start.2
  156.5 1.5 collective-permute-start.7
  158.0 6.4 %collective-permute-done.2 = bf16[8,128,128]{2,1,0:T(8,128)(2,1)S(1)} collective-permute-done((bf16[8,128,128]{2,1,0:T(8,128)(2,1)S(1)}, bf16[8,128,128]{2,1,0:T(8,128)(2,1)S(1)}, u32[]{:S(2)}, u32[]{:S(2)}) %collective-permute-start.2) | collective-permute-done | bytes 262176 | tf_op jit(solution)/shard_map/ppermute | solution.py:11
  164.9 6.8 %collective-permute-done.3 = bf16[8,128,128]{2,1,0:T(8,128)(2,1)S(1)} collective-permute-done((bf16[8,128,128]{2,1,0:T(8,128)(2,1)S(1)}, bf16[8,128,128]{2,1,0:T(8,128)(2,1)S(1)}, u32[]{:S(2)}, u32[]{:S(2)}) %collective-permute-start.3) | collective-permute-done | bytes 262176 | tf_op jit(solution)/shard_map/ppermute | solution.py:11
  172.9 6.8 %collective-permute-done.7 = bf16[8,3,128,128]{3,2,1,0:T(8,128)(2,1)S(1)} collective-permute-done((bf16[8,3,128,128]{3,2,1,0:T(8,128)(2,1)S(1)}, bf16[8,3,128,128]{3,2,1,0:T(8,128)(2,1)S(1)}, u32[]{:S(2)}, u32[]{:S(2)}) %collective-permute-start.7) | collective-permute-done | bytes 786464 | tf_op jit(solution)/shard_map/ppermute | solution.py:11
  180.6 12.1 %collective-permute-done.8 = bf16[8,2,128,128]{3,2,1,0:T(8,128)(2,1)S(1)} collective-permute-done((bf16[8,2,128,128]{3,2,1,0:T(8,128)(2,1)S(1)}, bf16[8,2,128,128]{3,2,1,0:T(8,128)(2,1)S(1)}, u32[]{:S(2)}, u32[]{:S(2)}) %collective-permute-start.8) | collective-permute-done | bytes 524320 | tf_op jit(solution)/shard_map/ppermute | solution.py:11
  192.9 1.9 collective-permute-start.9
  196.2 4.7 %collective-permute-done.9 = bf16[8,1,128,128]{3,2,1,0:T(8,128)(2,1)S(1)} collective-permute-done((bf16[8,1,128,128]{3,2,1,0:T(8,128)(2,1)S(1)}, bf16[8,1,128,128]{3,2,1,0:T(8,128)(2,1)S(1)}, u32[]{:S(2)}, u32[]{:S(2)}) %collective-permute-start.9) | collective-permute-done | bytes 262176 | tf_op jit(solution)/shard_map/ppermute | solution.py:11
  201.9 6.3 %convolution_convert_fusion = bf16[3072,2048]{1,0:T(8,128)(2,1)} fusion(bf16[256,3072]{0,1:T(8,128)(2,1)S(1)} %bitcast.132, bf16[1,256,2048]{2,1,0:T(8,128)(2,1)S(1)} %copy-done), kind=kOutput, calls=%fused_computation | convolution fusion | flops 3227516928 | bytes 15204352 | tf_op jit(solution)/shard_map/tr,tc->rc/dot_general | solution.py:117
  208.2 16.6 %copy.73 = bf16[2048,3,1024]{2,0,1:T(8,128)(2,1)} copy(bf16[2048,3,1024]{0,2,1:T(8,128)(2,1)} %bitcast.130) | data formatting | bytes 25165824 | tf_op jit(solution)/shard_map/convert_element_type | solution.py:119
  225.0 111.3 %reduce-scatter.2.cloned.1.call-done = bf16[64,3,1024]{2,0,1:T(8,128)(2,1)} async-done(((bf16[2048,3,1024]{2,0,1:T(8,128)(2,1)}), bf16[64,3,1024]{2,0,1:T(8,128)(2,1)}) %reduce-scatter.2.cloned.1.call-update) | async-done | bytes 393232 | tf_op jit(solution)/shard_map/reduce_scatter | solution.py:118
  336.3 2.4 fusion.1
  340.2 71.2 %all-reduce.2.cloned.1.call-done = bf16[64,3,1024]{2,0,1:T(8,128)(2,1)} async-done(((bf16[64,3,1024]{2,0,1:T(8,128)(2,1)}), bf16[64,3,1024]{2,0,1:T(8,128)(2,1)}) %all-reduce.2.cloned.1.call-update) | async-done | bytes 393232 | tf_op jit(solution)/shard_map/psum | solution.py:126
  411.5 2.0 convert_element_type.159
  (72 shorter events, 17.1 us)
Async XLA Ops:
  7.2 91.3 %copy-start = (bf16[1,256,2048]{2,1,0:T(8,128)(2,1)S(1)}, bf16[1,256,2048]{2,1,0:T(8,128)(2,1)}, u32[]{:S(2)}) copy-start(bf16[1,256,2048]{2,1,0:T(8,128)(2,1)} %param.5) | copy-start | bytes 3145732
  7.2 74.3 %all-gather.2.cloned.1.call-start = ((), (), s32[]{:S(2)}) async-start(), calls=%async_computation.1 | async-start | bytes 12976128 | tf_op jit(solution)/shard_map/all_gather | solution.py:65
  7.9 328.4 %reduce-scatter.2.cloned.1.call-start = ((), (), s32[]{:S(2)}) async-start(), calls=%async_computation.2 | async-start | bytes 12976128 | tf_op jit(solution)/shard_map/reduce_scatter | solution.py:118
  115.4 4.3 %collective-permute-start.5 = (bf16[8,5,128,128]{3,2,1,0:T(8,128)(2,1)}, bf16[8,5,128,128]{3,2,1,0:T(8,128)(2,1)}, u32[]{:S(2)}, u32[]{:S(2)}) collective-permute-start(bf16[8,5,128,128]{3,2,1,0:T(8,128)(2,1)} %get-tuple-element.23), channel_id=1, source_target_pairs={{0,8},{8,0},{16,24},{24,16},{32,40},{40,32},{48,56},{56,48},{64,72... | collective-permute-start | bytes 3932168 | tf_op jit(solution)/shard_map/ppermute | solution.py:11
  118.2 1.2 copy-start.4
  118.5 5.0 %collective-permute-start = (bf16[8,128,128]{2,1,0:T(8,128)(2,1)S(1)}, bf16[8,128,128]{2,1,0:T(8,128)(2,1)S(1)}, u32[]{:S(2)}, u32[]{:S(2)}) collective-permute-start(bf16[8,128,128]{2,1,0:T(8,128)(2,1)S(1)} %get-tuple-element.21), channel_id=1, source_target_pairs={{0,8},{8,0},{16,24},{24,16},{32,40},{40,32},{48,56},{56,48},{64,72... | collective-permute-start | bytes 786440 | tf_op jit(solution)/shard_map/ppermute | solution.py:11
  119.4 2.1 copy-start.2
  119.7 2.2 copy-start.1
  122.3 33.5 %collective-permute-start.6 = (bf16[8,4,128,128]{3,2,1,0:T(8,128)(2,1)S(1)}, bf16[8,4,128,128]{3,2,1,0:T(8,128)(2,1)S(1)}, u32[]{:S(2)}, u32[]{:S(2)}) collective-permute-start(bf16[8,4,128,128]{3,2,1,0:T(8,128)(2,1)S(1)} %pad_maximum_fusion.1), channel_id=1, source_target_pairs={{0,16},{8,24},{16,0},{24,8},{32,48},{40,56},{48,32},{56,40},{64,80... | collective-permute-start | bytes 3145736 | tf_op jit(solution)/shard_map/ppermute | solution.py:11
  123.6 29.8 %collective-permute-start.1 = (bf16[8,128,128]{2,1,0:T(8,128)(2,1)S(1)}, bf16[8,128,128]{2,1,0:T(8,128)(2,1)S(1)}, u32[]{:S(2)}, u32[]{:S(2)}) collective-permute-start(bf16[8,128,128]{2,1,0:T(8,128)(2,1)S(1)} %fusion.41), channel_id=1, source_target_pairs={{0,16},{8,24},{16,0},{24,8},{32,48},{40,56},{48,32},{56,40},{64,80... | collective-permute-start | bytes 786440 | tf_op jit(solution)/shard_map/ppermute | solution.py:11
  153.4 11.0 %collective-permute-start.2 = (bf16[8,128,128]{2,1,0:T(8,128)(2,1)S(1)}, bf16[8,128,128]{2,1,0:T(8,128)(2,1)S(1)}, u32[]{:S(2)}, u32[]{:S(2)}) collective-permute-start(bf16[8,128,128]{2,1,0:T(8,128)(2,1)S(1)} %fusion.61), channel_id=1, source_target_pairs={{0,32},{8,40},{16,48},{24,56},{32,0},{40,8},{48,16},{56,24},{64,96... | collective-permute-start | bytes 786440 | tf_op jit(solution)/shard_map/ppermute | solution.py:11
  156.5 23.2 %collective-permute-start.7 = (bf16[8,3,128,128]{3,2,1,0:T(8,128)(2,1)S(1)}, bf16[8,3,128,128]{3,2,1,0:T(8,128)(2,1)S(1)}, u32[]{:S(2)}, u32[]{:S(2)}) collective-permute-start(bf16[8,3,128,128]{3,2,1,0:T(8,128)(2,1)S(1)} %pad_maximum_fusion.2), channel_id=1, source_target_pairs={{0,32},{8,40},{16,48},{24,56},{32,0},{40,8},{48,16},{56,24},{64,96... | collective-permute-start | bytes 2359304 | tf_op jit(solution)/shard_map/ppermute | solution.py:11
  164.6 7.0 %collective-permute-start.3 = (bf16[8,128,128]{2,1,0:T(8,128)(2,1)S(1)}, bf16[8,128,128]{2,1,0:T(8,128)(2,1)S(1)}, u32[]{:S(2)}, u32[]{:S(2)}) collective-permute-start(bf16[8,128,128]{2,1,0:T(8,128)(2,1)S(1)} %fusion.42), channel_id=1, source_target_pairs={{0,64},{8,72},{16,80},{24,88},{32,96},{40,104},{48,112},{56,120},{... | collective-permute-start | bytes 786440 | tf_op jit(solution)/shard_map/ppermute | solution.py:11
  171.8 8.8 %collective-permute-start.4 = (bf16[8,128,128]{2,1,0:T(8,128)(2,1)S(1)}, bf16[8,128,128]{2,1,0:T(8,128)(2,1)S(1)}, u32[]{:S(2)}, u32[]{:S(2)}) collective-permute-start(bf16[8,128,128]{2,1,0:T(8,128)(2,1)S(1)} %add_convert_fusion), channel_id=1, source_target_pairs={{0,128},{8,136},{16,144},{24,152},{32,160},{40,168},{48,176},{56,1... | collective-permute-start | bytes 786440 | tf_op jit(solution)/shard_map/ppermute | solution.py:11
  180.2 12.4 %collective-permute-start.8 = (bf16[8,2,128,128]{3,2,1,0:T(8,128)(2,1)S(1)}, bf16[8,2,128,128]{3,2,1,0:T(8,128)(2,1)S(1)}, u32[]{:S(2)}, u32[]{:S(2)}) collective-permute-start(bf16[8,2,128,128]{3,2,1,0:T(8,128)(2,1)S(1)} %pad_maximum_fusion.3), channel_id=1, source_target_pairs={{0,64},{8,72},{16,80},{24,88},{32,96},{40,104},{48,112},{56,120},{... | collective-permute-start | bytes 1572872 | tf_op jit(solution)/shard_map/ppermute | solution.py:11
  180.6 15.1 %copy-start.5 = (bf16[8,128,5,128]{3,1,0,2:T(8,128)(2,1)}, bf16[8,128,5,128]{3,1,0,2:T(8,128)(2,1)S(1)}, u32[]{:S(2)}) copy-start(bf16[8,128,5,128]{3,1,0,2:T(8,128)(2,1)S(1)} %bitcast_dynamic-update-slice_fusion) | copy-start | bytes 3932164
  192.9 8.0 %collective-permute-start.9 = (bf16[8,1,128,128]{3,2,1,0:T(8,128)(2,1)S(1)}, bf16[8,1,128,128]{3,2,1,0:T(8,128)(2,1)S(1)}, u32[]{:S(2)}, u32[]{:S(2)}) collective-permute-start(bf16[8,1,128,128]{3,2,1,0:T(8,128)(2,1)S(1)} %fusion.21), channel_id=1, source_target_pairs={{0,128},{8,136},{16,144},{24,152},{32,160},{40,168},{48,176},{56,1... | collective-permute-start | bytes 786440 | tf_op jit(solution)/shard_map/ppermute | solution.py:11
  224.9 186.6 %all-reduce.2.cloned.1.call-start = ((), (), s32[]{:S(2)}) async-start(), calls=%async_computation.3 | async-start | bytes 786432 | tf_op jit(solution)/shard_map/psum | solution.py:126
  336.3 2.4 copy-start.3
Sparse Core Ops, SparseCore 0:
  10.6 70.8 all-gather.1
  225.0 111.1 reduce-scatter.1
  338.7 72.7 all-reduce.1
where the time goes:
time: 421 us; the launch traced here: 420 us
  waiting for transfers between devices  319 us (76%)
  local copies, waits for them, and re-layouts  42.8 us (10%)
  matrix products  26 us (6%)
  between operations  14.1 us (3%)
  starting transfers between devices  10.3 us (2%)
  other arithmetic  7.66 us (2%)
    reduce_scatter x1, waiting for transfers between devices, per_device(): lax.psum_scatter(partial_value.reshape(lax.axis_size('seq') * shard_rows,...  111 us
    psum x1, waiting for transfers between devices, per_device(): grad_w = lax.psum(seq_sum, 'dp').astype(jnp.float32)  71.2 us
    all_gather x1, waiting for transfers between devices, per_device(): lax.all_gather(w_qkv, 'seq', axis=0, tiled=True)  71.2 us
    ppermute x10, waiting for transfers between devices, swapped(): return lax.ppermute(value, axis, pairs)  64.7 us
    all_gather x1, local copies, waits for them, and re-layouts, per_device(): lax.all_gather(w_qkv, 'seq', axis=0, tiled=True)  17 us
    convert_element_type x1, local copies, waits for them, and re-layouts, per_device(): partial_value.reshape(lax.axis_size('seq') * shard_rows, 3, inner_width)  16.6 us
    ppermute x10, starting transfers between devices, swapped(): return lax.ppermute(value, axis, pairs)  10.1 us
  transfers between devices with their start and end apart: 13, of which 9 were waited for; matrix products, arithmetic and copies ran while one was open for 4% of the time, Pallas kernels for 0%

commit v1 on v0

--- a/solution.py
+++ b/solution.py
@@ -123,7 +123,7 @@
         scatter_dimension=0,
         tiled=True,
     )
-    grad_w = lax.psum(seq_sum, "dp").astype(jnp.float32)
+    grad_w = jnp.sum(lax.all_gather(seq_sum, "dp"), axis=0).astype(jnp.float32)
     return (attn_out, grad_w)
 
 

time: 421 us -> 395 us (0.938)
  waiting for transfers between devices: 319 us -> 291 us
    psum x1 -> x0, waiting for transfers between devices: 71.2 us -> none  [per_device(): grad_w = lax.psum(seq_sum, 'dp').astype(jnp.float32)]
    all_gather x0 -> x1, waiting for transfers between devices: none -> 42.8 us  [per_device(): grad_w = jnp.sum(lax.all_gather(seq_sum, 'dp'), axis=0).astype(jnp.float32)]
where the time goes in v1:
time: 395 us; the launch traced here: 393 us
  waiting for transfers between devices  291 us (74%)
  local copies, waits for them, and re-layouts  42.8 us (11%)
  matrix products  26 us (7%)
  between operations  14.1 us (4%)
  starting transfers between devices  10.3 us (3%)
  other arithmetic  9.17 us (2%)
    reduce_scatter x1, waiting for transfers between devices, per_device(): lax.psum_scatter(partial_value.reshape(lax.axis_size('seq') * shard_rows,...  111 us
    all_gather x1, waiting for transfers between devices, per_device(): lax.all_gather(w_qkv, 'seq', axis=0, tiled=True)  71.2 us
    ppermute x10, waiting for transfers between devices, swapped(): return lax.ppermute(value, axis, pairs)  64.7 us
    all_gather x1, waiting for transfers between devices, per_device(): grad_w = jnp.sum(lax.all_gather(seq_sum, 'dp'), axis=0).astype(jnp.float32)  42.8 us
    all_gather x1, local copies, waits for them, and re-layouts, per_device(): lax.all_gather(w_qkv, 'seq', axis=0, tiled=True)  17 us
    convert_element_type x1, local copies, waits for them, and re-layouts, per_device(): partial_value.reshape(lax.axis_size('seq') * shard_rows, 3, inner_width)  16.6 us
    ppermute x10, starting transfers between devices, swapped(): return lax.ppermute(value, axis, pairs)  10.1 us
    dot_general x1, matrix products, make_adder(): return jnp.dot(inputs, flat_rows, preferred_element_type=jnp.float32)  8.02 us
  transfers between devices with their start and end apart: 13, of which 9 were waited for; matrix products, arithmetic and copies ran while one was open for 4% of the time, Pallas kernels for 0%

profile of v1, /device:TPU:2, one launch (start us, length us, event | category | flops | bytes accessed | tf_op | source)
XLA Modules:
  0.0 393.0 jit_solution(8958609163809156113)
XLA Ops:
  9.2 1.1 copy.95
  10.4 71.2 %all-gather.4.cloned.1.call-done = bf16[2048,3,1024]{2,0,1:T(8,128)(2,1)} async-done(((bf16[64,3,1024]{2,0,1:T(8,128)(2,1)}), bf16[2048,3,1024]{2,0,1:T(8,128)(2,1)}) %all-gather.4.cloned.1.call-update) | async-done | bytes 12582928 | tf_op jit(solution)/shard_map/all_gather | solution.py:65
  81.5 17.0 %copy.51 = bf16[2048,3,1024]{0,2,1:T(8,128)(2,1)} copy(bf16[2048,3,1024]{2,0,1:T(8,128)(2,1)} %all-gather.4.cloned.1.call-done) | data formatting | bytes 25165824 | tf_op jit(solution)/shard_map/all_gather | solution.py:65
  98.5 8.0 %fusion.6 = bf16[32,8,24,128]{3,1,2,0:T(8,128)(2,1)S(1)} fusion(bf16[2048,3072]{0,1:T(8,128)(2,1)} %bitcast.132, bf16[1,256,2048]{2,1,0:T(8,128)(2,1)S(1)} %copy-done), kind=kOutput, calls=%fused_computation.14 | convolution fusion | flops 3222011904 | bytes 15204352 | tf_op jit(solution)/shard_map/dot_general | solution.py:30
  108.9 2.5 copy.67
  111.5 3.9 %fusion.67 = (bf16[8,5,128,128]{3,2,1,0:T(8,128)(2,1)}, f32[8,5,128,128]{3,2,1,0:T(8,128)}) fusion(bf16[256,8,128,1]{2,1,0,3:T(8,128)(2,1)S(1)} %bitcast.135, f32[256,8,128]{0,2,1:T(8,128)} %copy.67, f32[256,8,5]{0,2,1:T(8,128)S(1)} %copy.59), kind=kOutput, calls=%fused_computation.125 | convolution fusion | flops 338821120 | bytes 5545984 | tf_op jit(solution)/shard_map/thld,the->hlde/dot_general | solution.py:103
  116.8 1.3 copy.91
  119.7 1.8 convert_element_type.146
  123.6 1.5 collective-permute-start.1
  125.5 27.9 %collective-permute-done.1 = bf16[8,128,128]{2,1,0:T(8,128)(2,1)S(1)} collective-permute-done((bf16[8,128,128]{2,1,0:T(8,128)(2,1)S(1)}, bf16[8,128,128]{2,1,0:T(8,128)(2,1)S(1)}, u32[]{:S(2)}, u32[]{:S(2)}) %collective-permute-start.1) | collective-permute-done | bytes 262176 | tf_op jit(solution)/shard_map/ppermute | solution.py:11
  153.4 2.4 collective-permute-start.2
  156.5 1.5 collective-permute-start.7
  158.0 6.4 %collective-permute-done.2 = bf16[8,128,128]{2,1,0:T(8,128)(2,1)S(1)} collective-permute-done((bf16[8,128,128]{2,1,0:T(8,128)(2,1)S(1)}, bf16[8,128,128]{2,1,0:T(8,128)(2,1)S(1)}, u32[]{:S(2)}, u32[]{:S(2)}) %collective-permute-start.2) | collective-permute-done | bytes 262176 | tf_op jit(solution)/shard_map/ppermute | solution.py:11
  164.9 6.8 %collective-permute-done.3 = bf16[8,128,128]{2,1,0:T(8,128)(2,1)S(1)} collective-permute-done((bf16[8,128,128]{2,1,0:T(8,128)(2,1)S(1)}, bf16[8,128,128]{2,1,0:T(8,128)(2,1)S(1)}, u32[]{:S(2)}, u32[]{:S(2)}) %collective-permute-start.3) | collective-permute-done | bytes 262176 | tf_op jit(solution)/shard_map/ppermute | solution.py:11
  172.9 6.8 %collective-permute-done.7 = bf16[8,3,128,128]{3,2,1,0:T(8,128)(2,1)S(1)} collective-permute-done((bf16[8,3,128,128]{3,2,1,0:T(8,128)(2,1)S(1)}, bf16[8,3,128,128]{3,2,1,0:T(8,128)(2,1)S(1)}, u32[]{:S(2)}, u32[]{:S(2)}) %collective-permute-start.7) | collective-permute-done | bytes 786464 | tf_op jit(solution)/shard_map/ppermute | solution.py:11
  180.6 12.1 %collective-permute-done.8 = bf16[8,2,128,128]{3,2,1,0:T(8,128)(2,1)S(1)} collective-permute-done((bf16[8,2,128,128]{3,2,1,0:T(8,128)(2,1)S(1)}, bf16[8,2,128,128]{3,2,1,0:T(8,128)(2,1)S(1)}, u32[]{:S(2)}, u32[]{:S(2)}) %collective-permute-start.8) | collective-permute-done | bytes 524320 | tf_op jit(solution)/shard_map/ppermute | solution.py:11
  192.9 1.9 collective-permute-start.9
  196.2 4.7 %collective-permute-done.9 = bf16[8,1,128,128]{3,2,1,0:T(8,128)(2,1)S(1)} collective-permute-done((bf16[8,1,128,128]{3,2,1,0:T(8,128)(2,1)S(1)}, bf16[8,1,128,128]{3,2,1,0:T(8,128)(2,1)S(1)}, u32[]{:S(2)}, u32[]{:S(2)}) %collective-permute-start.9) | collective-permute-done | bytes 262176 | tf_op jit(solution)/shard_map/ppermute | solution.py:11
  201.9 6.3 %convolution_convert_fusion = bf16[3072,2048]{1,0:T(8,128)(2,1)} fusion(bf16[256,3072]{0,1:T(8,128)(2,1)S(1)} %bitcast.133, bf16[1,256,2048]{2,1,0:T(8,128)(2,1)S(1)} %copy-done), kind=kOutput, calls=%fused_computation | convolution fusion | flops 3227516928 | bytes 15204352 | tf_op jit(solution)/shard_map/tr,tc->rc/dot_general | solution.py:117
  208.2 16.6 %copy.72 = bf16[2048,3,1024]{2,0,1:T(8,128)(2,1)} copy(bf16[2048,3,1024]{0,2,1:T(8,128)(2,1)} %bitcast.131) | data formatting | bytes 25165824 | tf_op jit(solution)/shard_map/convert_element_type | solution.py:119
  225.0 111.3 %reduce-scatter.2.cloned.1.call-done = bf16[64,3,1024]{2,0,1:T(8,128)(2,1)} async-done(((bf16[2048,3,1024]{2,0,1:T(8,128)(2,1)}), bf16[64,3,1024]{2,0,1:T(8,128)(2,1)}) %reduce-scatter.2.cloned.1.call-update) | async-done | bytes 393232 | tf_op jit(solution)/shard_map/reduce_scatter | solution.py:118
  336.3 2.4 fusion.1
  340.2 42.8 %all-gather.6.cloned.1.call-done = bf16[512,3,1024]{2,0,1:T(8,128)(2,1)} async-done(((bf16[64,3,1024]{2,0,1:T(8,128)(2,1)}), bf16[512,3,1024]{2,0,1:T(8,128)(2,1)}) %all-gather.6.cloned.1.call-update) | async-done | bytes 3145744 | tf_op jit(solution)/shard_map/all_gather | solution.py:126
  383.0 2.5 reduce_sum.32
  (73 shorter events, 18.1 us)
Async XLA Ops:
  7.2 91.3 %copy-start = (bf16[1,256,2048]{2,1,0:T(8,128)(2,1)S(1)}, bf16[1,256,2048]{2,1,0:T(8,128)(2,1)}, u32[]{:S(2)}) copy-start(bf16[1,256,2048]{2,1,0:T(8,128)(2,1)} %param.5) | copy-start | bytes 3145732
  7.2 74.3 %all-gather.4.cloned.1.call-start = ((), (), s32[]{:S(2)}) async-start(), calls=%async_computation.1 | async-start | bytes 12976128 | tf_op jit(solution)/shard_map/all_gather | solution.py:65
  7.9 328.4 %reduce-scatter.2.cloned.1.call-start = ((), (), s32[]{:S(2)}) async-start(), calls=%async_computation.2 | async-start | bytes 12976128 | tf_op jit(solution)/shard_map/reduce_scatter | solution.py:118
  115.4 4.3 %collective-permute-start.5 = (bf16[8,5,128,128]{3,2,1,0:T(8,128)(2,1)}, bf16[8,5,128,128]{3,2,1,0:T(8,128)(2,1)}, u32[]{:S(2)}, u32[]{:S(2)}) collective-permute-start(bf16[8,5,128,128]{3,2,1,0:T(8,128)(2,1)} %get-tuple-element.23), channel_id=1, source_target_pairs={{0,8},{8,0},{16,24},{24,16},{32,40},{40,32},{48,56},{56,48},{64,72... | collective-permute-start | bytes 3932168 | tf_op jit(solution)/shard_map/ppermute | solution.py:11
  118.2 1.2 copy-start.4
  118.5 5.0 %collective-permute-start = (bf16[8,128,128]{2,1,0:T(8,128)(2,1)S(1)}, bf16[8,128,128]{2,1,0:T(8,128)(2,1)S(1)}, u32[]{:S(2)}, u32[]{:S(2)}) collective-permute-start(bf16[8,128,128]{2,1,0:T(8,128)(2,1)S(1)} %get-tuple-element.21), channel_id=1, source_target_pairs={{0,8},{8,0},{16,24},{24,16},{32,40},{40,32},{48,56},{56,48},{64,72... | collective-permute-start | bytes 786440 | tf_op jit(solution)/shard_map/ppermute | solution.py:11
  119.4 2.1 copy-start.2
  119.7 2.2 copy-start.1
  122.3 33.5 %collective-permute-start.6 = (bf16[8,4,128,128]{3,2,1,0:T(8,128)(2,1)S(1)}, bf16[8,4,128,128]{3,2,1,0:T(8,128)(2,1)S(1)}, u32[]{:S(2)}, u32[]{:S(2)}) collective-permute-start(bf16[8,4,128,128]{3,2,1,0:T(8,128)(2,1)S(1)} %pad_maximum_fusion.1), channel_id=1, source_target_pairs={{0,16},{8,24},{16,0},{24,8},{32,48},{40,56},{48,32},{56,40},{64,80... | collective-permute-start | bytes 3145736 | tf_op jit(solution)/shard_map/ppermute | solution.py:11
  123.6 29.8 %collective-permute-start.1 = (bf16[8,128,128]{2,1,0:T(8,128)(2,1)S(1)}, bf16[8,128,128]{2,1,0:T(8,128)(2,1)S(1)}, u32[]{:S(2)}, u32[]{:S(2)}) collective-permute-start(bf16[8,128,128]{2,1,0:T(8,128)(2,1)S(1)} %fusion.41), channel_id=1, source_target_pairs={{0,16},{8,24},{16,0},{24,8},{32,48},{40,56},{48,32},{56,40},{64,80... | collective-permute-start | bytes 786440 | tf_op jit(solution)/shard_map/ppermute | solution.py:11
  153.4 11.0 %collective-permute-start.2 = (bf16[8,128,128]{2,1,0:T(8,128)(2,1)S(1)}, bf16[8,128,128]{2,1,0:T(8,128)(2,1)S(1)}, u32[]{:S(2)}, u32[]{:S(2)}) collective-permute-start(bf16[8,128,128]{2,1,0:T(8,128)(2,1)S(1)} %fusion.61), channel_id=1, source_target_pairs={{0,32},{8,40},{16,48},{24,56},{32,0},{40,8},{48,16},{56,24},{64,96... | collective-permute-start | bytes 786440 | tf_op jit(solution)/shard_map/ppermute | solution.py:11
  156.5 23.2 %collective-permute-start.7 = (bf16[8,3,128,128]{3,2,1,0:T(8,128)(2,1)S(1)}, bf16[8,3,128,128]{3,2,1,0:T(8,128)(2,1)S(1)}, u32[]{:S(2)}, u32[]{:S(2)}) collective-permute-start(bf16[8,3,128,128]{3,2,1,0:T(8,128)(2,1)S(1)} %pad_maximum_fusion.2), channel_id=1, source_target_pairs={{0,32},{8,40},{16,48},{24,56},{32,0},{40,8},{48,16},{56,24},{64,96... | collective-permute-start | bytes 2359304 | tf_op jit(solution)/shard_map/ppermute | solution.py:11
  164.6 7.0 %collective-permute-start.3 = (bf16[8,128,128]{2,1,0:T(8,128)(2,1)S(1)}, bf16[8,128,128]{2,1,0:T(8,128)(2,1)S(1)}, u32[]{:S(2)}, u32[]{:S(2)}) collective-permute-start(bf16[8,128,128]{2,1,0:T(8,128)(2,1)S(1)} %fusion.42), channel_id=1, source_target_pairs={{0,64},{8,72},{16,80},{24,88},{32,96},{40,104},{48,112},{56,120},{... | collective-permute-start | bytes 786440 | tf_op jit(solution)/shard_map/ppermute | solution.py:11
  171.8 8.8 %collective-permute-start.4 = (bf16[8,128,128]{2,1,0:T(8,128)(2,1)S(1)}, bf16[8,128,128]{2,1,0:T(8,128)(2,1)S(1)}, u32[]{:S(2)}, u32[]{:S(2)}) collective-permute-start(bf16[8,128,128]{2,1,0:T(8,128)(2,1)S(1)} %add_convert_fusion), channel_id=1, source_target_pairs={{0,128},{8,136},{16,144},{24,152},{32,160},{40,168},{48,176},{56,1... | collective-permute-start | bytes 786440 | tf_op jit(solution)/shard_map/ppermute | solution.py:11
  180.2 12.4 %collective-permute-start.8 = (bf16[8,2,128,128]{3,2,1,0:T(8,128)(2,1)S(1)}, bf16[8,2,128,128]{3,2,1,0:T(8,128)(2,1)S(1)}, u32[]{:S(2)}, u32[]{:S(2)}) collective-permute-start(bf16[8,2,128,128]{3,2,1,0:T(8,128)(2,1)S(1)} %pad_maximum_fusion.3), channel_id=1, source_target_pairs={{0,64},{8,72},{16,80},{24,88},{32,96},{40,104},{48,112},{56,120},{... | collective-permute-start | bytes 1572872 | tf_op jit(solution)/shard_map/ppermute | solution.py:11
  180.6 15.1 %copy-start.5 = (bf16[8,128,5,128]{3,1,0,2:T(8,128)(2,1)}, bf16[8,128,5,128]{3,1,0,2:T(8,128)(2,1)S(1)}, u32[]{:S(2)}) copy-start(bf16[8,128,5,128]{3,1,0,2:T(8,128)(2,1)S(1)} %bitcast_dynamic-update-slice_fusion) | copy-start | bytes 3932164
  192.9 8.0 %collective-permute-start.9 = (bf16[8,1,128,128]{3,2,1,0:T(8,128)(2,1)S(1)}, bf16[8,1,128,128]{3,2,1,0:T(8,128)(2,1)S(1)}, u32[]{:S(2)}, u32[]{:S(2)}) collective-permute-start(bf16[8,1,128,128]{3,2,1,0:T(8,128)(2,1)S(1)} %fusion.21), channel_id=1, source_target_pairs={{0,128},{8,136},{16,144},{24,152},{32,160},{40,168},{48,176},{56,1... | collective-permute-start | bytes 786440 | tf_op jit(solution)/shard_map/ppermute | solution.py:11
  224.9 158.1 %all-gather.6.cloned.1.call-start = ((), (), s32[]{:S(2)}) async-start(), calls=%async_computation.3 | async-start | bytes 3538944 | tf_op jit(solution)/shard_map/all_gather | solution.py:126
  336.3 2.4 copy-start.3
Sparse Core Ops, SparseCore 0:
  10.6 70.8 all-gather.3
  225.0 111.1 reduce-scatter.1
  338.2 44.7 all-gather.5
